TPU v7x, 256 devices: a whole 4x4x8 slice. The times are simulated.
256 devices in a mesh: seq: 16 (over x, y), chan: 4 (over z_hi, core), dp: 4 (over z_lo).
Axes of the slice: x: 4, y: 4, z: 8 (z_hi: 2, z_lo: 4; z = z_hi * 4 + z_lo), core: 2. Of those that a mesh axis runs over, the one named last changes fastest.
Arguments:
- inputs: bfloat16 [4, 4096, 1024], P('dp', 'seq', 'chan'), may hold values from -0.046875 to 0.046875
- grad_out: bfloat16 [4, 4096, 1024], P('dp', 'seq', 'chan'), may hold values from -6 to 6
- kernel: float32 [4096, 1024], P('seq', ('chan', 'dp')), may hold values from -0.09375 to 0.09375
- skip: float32 [1024], P('chan'), may hold values from 0.5 to 1.5
Outputs:
- grad_inputs: bfloat16 [4, 4096, 1024], P('dp', 'seq', 'chan')
- grad_kernel: float32 [4096, 1024], P('seq', ('chan', 'dp'))
All inputs are finite; a program needn't handle non-finite values.
Results may differ from a plain program's by a relative error of at most 0.001.
Values may be sent and summed in bfloat16 or wider, within the bound.
No kernel may reach another device: no remote copies, remote signals or barrier semaphores. Data moves between devices by JAX's collectives and lax.ppermute only.
A program may use at most 64 MiB of HBM per device.

v0:
```python
import jax
import jax.numpy as jnp
from jax import lax
from jax.experimental import pallas as pl
from jax.experimental.pallas import tpu as pltpu
from jax.sharding import PartitionSpec as P

F32 = jnp.float32
BF16 = jnp.bfloat16
GROUP = ("seq", "dp")
LANES = 128
ROWS_OUT = 8
ROWS_BACK = 8


def take(stage, first, count, stride, blocks):
    return jnp.concatenate([stage[b, pl.ds(first, count, stride=stride), :] for b in blocks], axis=1)


def put(stage, first, stride, values, blocks):
    for at, b in enumerate(blocks):
        part = values[:, at * LANES : (at + 1) * LANES]
        stage[b, pl.ds(first, values.shape[0], stride=stride), :] = part


def load_all(stage, ref):
    values = ref[...].astype(F32).reshape(stage.shape[1], -1)
    for b in range(stage.shape[0]):
        stage[b] = values[:, b * LANES : (b + 1) * LANES]


def store_all(ref, stage):
    values = jnp.concatenate([stage[b] for b in range(stage.shape[0])], axis=1)
    ref[...] = values.astype(BF16).reshape(ref.shape)


def pack_kernel(u_ref, g_ref, k_ref, send_ref, stage):
    peers = send_ref.shape[0]
    piece, channels = g_ref.shape
    per_peer = channels // peers
    g_rows = g_ref[...].astype(F32).T
    u_rows = u_ref[...].astype(F32).T
    for e in range(per_peer):
        rows = slice(e * peers, (e + 1) * peers)
        put(stage, e, ROWS_OUT, g_rows[rows], (0, 1))
        put(stage, per_peer + e, ROWS_OUT, u_rows[rows], (0, 1))
    k_rows = k_ref[...].T
    high = k_rows.astype(BF16).astype(F32)
    low = k_rows - high
    for part, values in enumerate((high, low)):
        for half in range(2):
            put(stage, 2 * part + half, ROWS_OUT, values[:, half * LANES : (half + 1) * LANES], (2,))
    for row in range(4, ROWS_OUT):
        put(stage, row, ROWS_OUT, jnp.zeros((peers, LANES), F32), (2,))
    store_all(send_ref, stage)


def correlate_kernel(place_ref, skip_ref, recv_ref, back_ref, stage, shifted, hankel, toeplitz, kgrad, out):
    peers = recv_ref.shape[0]
    pieces, piece, per_peer = 16, 256, 4
    batch = peers // pieces
    place = place_ref[0]
    load_all(stage, recv_ref)
    row_ids = lax.broadcasted_iota(jnp.int32, (LANES, LANES), 0)
    col_ids = lax.broadcasted_iota(jnp.int32, (LANES, LANES), 1)
    on_or_after = col_ids >= row_ids
    after = col_ids > row_ids
    backwards = jnp.where(row_ids + col_ids == LANES - 1, 1.0, 0.0).astype(BF16)
    shifted[:, peers:, :] = jnp.zeros((2, peers, piece), F32)
    for e in range(per_peer):
        g_blocks = take(stage, e, peers, ROWS_OUT, (0, 1))
        u_blocks = take(stage, per_peer + e, peers, ROWS_OUT, (0, 1))
        shifted[0, 0:peers, :] = g_blocks
        shifted[1, 0:peers, 0:LANES] = g_blocks[:, LANES:]
        shifted[1, 0:peers, LANES:] = shifted[0, batch : peers + batch, 0:LANES]
        for step in range(pieces):
            for half in range(2):
                hankel[half * peers : (half + 1) * peers, step * piece : (step + 1) * piece] = shifted[
                    half, batch * step : batch * step + peers, :
                ].astype(BF16)
        first = per_peer * ROWS_OUT
        halves = [
            take(stage, e * ROWS_OUT + half, pieces, first, (2,))
            + take(stage, e * ROWS_OUT + 2 + half, pieces, first, (2,))
            for half in range(2)
        ]
        before = jnp.zeros((LANES, LANES), F32)
        for block in range(2 * pieces):
            values = halves[block % 2][block // 2 : block // 2 + 1, :]
            turned = pltpu.roll(jnp.broadcast_to(values, (LANES, LANES)), 0, 1, stride=1, stride_axis=0)
            square = jnp.where(on_or_after, turned, before)
            before = turned
            high = square.astype(BF16)
            columns = slice(block * LANES, (block + 1) * LANES)
            toeplitz[0:LANES, columns] = high
            toeplitz[LANES:, columns] = (square - high.astype(F32)).astype(BF16)
        both = lax.dot_general(
            hankel[...], toeplitz[...], (((1,), (1,)), ((), ())), preferred_element_type=F32
        )
        conv = both[:, 0:LANES] + both[:, LANES:]
        conv = jnp.concatenate([conv[0:peers], conv[peers:]], axis=1)
        gain = skip_ref[e * peers + place]
        put(out, e, ROWS_BACK, conv + gain * g_blocks, (0, 1))
        u_stack = jnp.concatenate([u_blocks[:, 0:LANES], u_blocks[:, LANES:]], axis=0).astype(BF16)
        u_turned = lax.dot_general(
            backwards, u_stack, (((1,), (1,)), ((), ())), preferred_element_type=F32
        ).astype(BF16)
        later = jnp.zeros((LANES, LANES), F32)
        for block in range(2 * pieces - 1, -1, -1):
            columns = slice(block * LANES, (block + 1) * LANES)
            products = jnp.dot(u_turned, hankel[:, columns], preferred_element_type=F32)
            turned = pltpu.roll(products, 1, 1, stride=1, stride_axis=0)
            lags = jnp.sum(jnp.where(after, later, turned), axis=0, keepdims=True)
            later = turned
            place_in = (block // 2) * per_peer + e
            half = block % 2
            kgrad[place_in : place_in + 1, half * LANES : (half + 1) * LANES] = lags
    lags = kgrad[...]
    high = lags.astype(BF16).astype(F32)
    put(out, per_peer, ROWS_BACK, high, (0, 1))
    put(out, per_peer + 1, ROWS_BACK, lags - high, (0, 1))
    for row in range(per_peer + 2, ROWS_BACK):
        put(out, row, ROWS_BACK, jnp.zeros((peers, piece), F32), (0, 1))
    store_all(back_ref, out)


def unpack_kernel(recv_ref, grad_inputs_ref, grad_kernel_ref, stage):
    peers = recv_ref.shape[0]
    per_peer = grad_inputs_ref.shape[1] // peers
    load_all(stage, recv_ref)
    rows = jnp.concatenate(
        [take(stage, e, peers, ROWS_BACK, (0, 1)) for e in range(per_peer)], axis=0
    )
    grad_inputs_ref[...] = rows.T.astype(BF16)
    lags = take(stage, per_peer, peers, ROWS_BACK, (0, 1)) + take(
        stage, per_peer + 1, peers, ROWS_BACK, (0, 1)
    )
    grad_kernel_ref[...] = lags.T


def shards(inputs, grad_out, kernel, skip):
    peers = lax.axis_size(GROUP)
    _, piece, channels = inputs.shape
    vmem = pl.BlockSpec(memory_space=pltpu.VMEM)
    smem = pl.BlockSpec(memory_space=pltpu.SMEM)
    params = pltpu.CompilerParams(vmem_limit_bytes=40 * 2**20)
    send = pl.pallas_call(
        pack_kernel,
        out_shape=jax.ShapeDtypeStruct((peers, ROWS_OUT, piece + LANES), BF16),
        in_specs=[vmem] * 3,
        out_specs=vmem,
        scratch_shapes=[pltpu.VMEM((3, peers * ROWS_OUT, LANES), F32)],
        compiler_params=params,
    )(inputs[0], grad_out[0], kernel)
    recv = lax.all_to_all(send, GROUP, 0, 0, tiled=True)
    place = lax.axis_index(GROUP).astype(jnp.int32).reshape(1)
    back = pl.pallas_call(
        correlate_kernel,
        out_shape=jax.ShapeDtypeStruct((peers, ROWS_BACK, piece), BF16),
        in_specs=[smem, smem, vmem],
        out_specs=vmem,
        scratch_shapes=[
            pltpu.VMEM((3, peers * ROWS_OUT, LANES), F32),
            pltpu.VMEM((2, 2 * peers, piece), F32),
            pltpu.VMEM((2 * peers, 4096), BF16),
            pltpu.VMEM((2 * LANES, 4096), BF16),
            pltpu.VMEM((peers, piece), F32),
            pltpu.VMEM((2, peers * ROWS_BACK, LANES), F32),
        ],
        compiler_params=params,
    )(place, skip, recv)
    landed = lax.all_to_all(back, GROUP, 0, 0, tiled=True)
    grad_inputs, grad_kernel = pl.pallas_call(
        unpack_kernel,
        out_shape=(
            jax.ShapeDtypeStruct((piece, channels), BF16),
            jax.ShapeDtypeStruct(kernel.shape, F32),
        ),
        in_specs=[vmem],
        out_specs=(vmem, vmem),
        scratch_shapes=[pltpu.VMEM((2, peers * ROWS_BACK, LANES), F32)],
        compiler_params=params,
    )(landed)
    return (grad_inputs[None], grad_kernel)


def solution(mesh):
    in_specs = (P("dp", "seq", "chan"), P("dp", "seq", "chan"), P("seq", ("chan", "dp")), P("chan"))
    out_specs = (P("dp", "seq", "chan"), P("seq", ("chan", "dp")))
    return jax.shard_map(shards, mesh=mesh, in_specs=in_specs, out_specs=out_specs, check_vma=False)
```

profile of v0, /device:TPU:32, one launch (start us, length us, event | category | flops | bytes accessed | tf_op | source)
XLA Modules:
  0.0 54.5 jit_solution(5538850436489269743)
XLA Ops:
  0.6 0.0 copy-start
  0.6 1.0 %copy.6.k_ref = f32[256,64]{1,0:T(8,128)S(1)} copy(f32[256,64]{0,1:T(8,128)} %param.6) | data formatting | bytes 131072 | tf_op args[2]
  1.6 0.0 copy-done
  1.6 0.0 copy-start.1
  1.6 0.9 %copy-done.1 = bf16[1,256,256]{2,1,0:T(8,128)(2,1)S(1)} copy-done((bf16[1,256,256]{2,1,0:T(8,128)(2,1)S(1)}, bf16[1,256,256]{2,1,0:T(8,128)(2,1)}, u32[]{:S(2)}) %copy-start.1) | copy-done | bytes 131096
  2.5 1.0 %shard_map.59 = bf16[64,8,384]{2,1,0:T(8,128)(2,1)} custom-call(bf16[256,256]{1,0:T(8,128)(2,1)S(1)} %bitcast.4, bf16[256,256]{1,0:T(8,128)(2,1)S(1)} %bitcast.5, f32[256,64]{1,0:T(8,128)S(1)} %copy.6.k_ref), custom_call_target="tpu_custom_call" | custom-call | tf_op jit(solution)/shard_map/pallas_call | solution.py:147
  3.5 11.7 %all-to-all-start = ((bf16[64,8,384]{2,1,0:T(8,128)(2,1)}), bf16[64,8,384]{2,1,0:T(8,128)(2,1)S(1)}, u32[]{:S(2)}, u32[]{:S(2)}) async-start(bf16[64,8,384]{2,1,0:T(8,128)(2,1)} %shard_map.59), calls=%async_computation | async-start | bytes 786432 | tf_op jit(solution)/shard_map/all_to_all | solution.py:155
  15.1 0.0 copy-start.2
  15.2 14.5 %all-to-all-done.recv_ref = bf16[64,8,384]{2,1,0:T(8,128)(2,1)S(1)} async-done(((bf16[64,8,384]{2,1,0:T(8,128)(2,1)}), bf16[64,8,384]{2,1,0:T(8,128)(2,1)S(1)}, u32[]{:S(2)}, u32[]{:S(2)}) %all-to-all-start) | async-done | bytes 393248 | tf_op jit(solution)/shard_map/all_to_all | solution.py:155
  29.7 0.0 copy-done.2
  29.7 6.4 %shard_map.60 = bf16[64,8,256]{2,1,0:T(8,128)(2,1)S(1)} custom-call(s32[1]{0:T(128)} %bitcast.place_ref, f32[256]{0:T(256)S(1)} %copy-done.2, bf16[64,8,384]{2,1,0:T(8,128)(2,1)S(1)} %all-to-all-done.recv_ref), custom_call_target="tpu_custom_call" | custom-call | tf_op jit(solution)/shard_map/pallas_call | solution.py:157
  36.1 16.9 %all_to_all.10.recv_ref = bf16[64,8,256]{2,1,0:T(8,128)(2,1)S(1)} all-to-all(bf16[64,8,256]{2,1,0:T(8,128)(2,1)S(1)} %shard_map.60), channel_id=1, replica_groups=mesh['seq'=16,'chan'=4,'dp'=4] {'seq','dp'}, dimensions={0} | all-to-all | bytes 524288 | tf_op jit(solution)/shard_map/all_to_all | solution.py:172
  53.0 0.8 %shard_map.61 = (bf16[256,256]{1,0:T(8,128)(2,1)}, f32[256,64]{1,0:T(8,128)S(1)}) custom-call(bf16[64,8,256]{2,1,0:T(8,128)(2,1)S(1)} %all_to_all.10.recv_ref), custom_call_target="tpu_custom_call" | custom-call | tf_op jit(solution)/shard_map/pallas_call | solution.py:173
  53.7 0.7 %copy.7 = f32[256,64]{0,1:T(8,128)} copy(f32[256,64]{1,0:T(8,128)S(1)} %get-tuple-element.7) | data formatting | bytes 131072
Async XLA Ops:
  0.6 1.0 %copy-start = (bf16[1,256,256]{2,1,0:T(8,128)(2,1)S(1)}, bf16[1,256,256]{2,1,0:T(8,128)(2,1)}, u32[]{:S(2)}) copy-start(bf16[1,256,256]{2,1,0:T(8,128)(2,1)} %param.4) | copy-start | bytes 393220
  1.6 0.9 %copy-start.1 = (bf16[1,256,256]{2,1,0:T(8,128)(2,1)S(1)}, bf16[1,256,256]{2,1,0:T(8,128)(2,1)}, u32[]{:S(2)}) copy-start(bf16[1,256,256]{2,1,0:T(8,128)(2,1)} %param.5) | copy-start | bytes 393220
  3.5 26.2 %all-to-all-start = ((bf16[64,8,384]{2,1,0:T(8,128)(2,1)}), bf16[64,8,384]{2,1,0:T(8,128)(2,1)S(1)}, u32[]{:S(2)}, u32[]{:S(2)}) async-start(bf16[64,8,384]{2,1,0:T(8,128)(2,1)} %shard_map.59), calls=%async_computation | async-start | bytes 786432 | tf_op jit(solution)/shard_map/all_to_all | solution.py:155
  15.1 14.6 %copy-start.2 = (f32[256]{0:T(256)S(1)}, f32[256]{0:T(256)}, u32[]{:S(2)}) copy-start(f32[256]{0:T(256)} %skip_ref.1) | copy-start | bytes 3076
where the time goes:
time: 55.1 us; the launch traced here: 54.5 us
  blocking collectives  16.9 us (31%)
  waiting for transfers between devices  14.5 us (26%)
  starting transfers between devices  11.7 us (21%)
  Pallas kernels  8.12 us (15%)
  local copies, waits for them, and re-layouts  2.59 us (5%)
  between operations  0.69 us (1%)
    all_to_all x1, blocking collectives, shards(): landed = lax.all_to_all(back, GROUP, 0, 0, tiled=True)  16.9 us
    all_to_all x1, waiting for transfers between devices, shards(): recv = lax.all_to_all(send, GROUP, 0, 0, tiled=True)  14.5 us
    all_to_all x1, starting transfers between devices, shards(): recv = lax.all_to_all(send, GROUP, 0, 0, tiled=True)  11.7 us
    pallas_call x1, Pallas kernels, shards(): pl.pallas_call(correlate_kernel, out_shape=jax.ShapeDtypeStruct((peers, R...  6.37 us
    unnamed x8, local copies, waits for them, and re-layouts  2.59 us
  transfers between devices with their start and end apart: 1, of which 1 were waited for; matrix products, arithmetic and copies ran while one was open for 0% of the time, Pallas kernels for 0%

commit v1 on v0

--- a/solution.py
+++ b/solution.py
@@ -9,8 +9,7 @@
 BF16 = jnp.bfloat16
 GROUP = ("seq", "dp")
 LANES = 128
-ROWS_OUT = 8
-ROWS_BACK = 8
+OWN = 4
 
 
 def take(stage, first, count, stride, blocks):
@@ -31,27 +30,29 @@
 
 def store_all(ref, stage):
     values = jnp.concatenate([stage[b] for b in range(stage.shape[0])], axis=1)
-    ref[...] = values.astype(BF16).reshape(ref.shape)
+    ref[...] = values.reshape(ref.shape).astype(BF16)
 
 
-def pack_kernel(u_ref, g_ref, k_ref, send_ref, stage):
+def pack_kernel(u_hbm, g_hbm, k_hbm, send_ref, u_ref, g_ref, k_ref, stage, sems):
+    copies = [
+        pltpu.make_async_copy(src, dst, sems.at[at])
+        for at, (src, dst) in enumerate(((k_hbm, k_ref), (g_hbm, g_ref), (u_hbm, u_ref)))
+    ]
+    for copy in copies:
+        copy.start()
     peers = send_ref.shape[0]
-    piece, channels = g_ref.shape
-    per_peer = channels // peers
-    g_rows = g_ref[...].astype(F32).T
-    u_rows = u_ref[...].astype(F32).T
-    for e in range(per_peer):
-        rows = slice(e * peers, (e + 1) * peers)
-        put(stage, e, ROWS_OUT, g_rows[rows], (0, 1))
-        put(stage, per_peer + e, ROWS_OUT, u_rows[rows], (0, 1))
-    k_rows = k_ref[...].T
+    copies[0].wait()
+    k_rows = k_ref[...]
     high = k_rows.astype(BF16).astype(F32)
     low = k_rows - high
     for part, values in enumerate((high, low)):
         for half in range(2):
-            put(stage, 2 * part + half, ROWS_OUT, values[:, half * LANES : (half + 1) * LANES], (2,))
-    for row in range(4, ROWS_OUT):
-        put(stage, row, ROWS_OUT, jnp.zeros((peers, LANES), F32), (2,))
+            put(stage, 2 * part + half, OWN, values[:, half * LANES : (half + 1) * LANES], (4,))
+    for at, ref in ((1, g_ref), (2, u_ref)):
+        copies[at].wait()
+        rows = ref[...].astype(F32).T
+        for e in range(OWN):
+            put(stage, e, OWN, rows[e * peers : (e + 1) * peers], (2 * at - 2, 2 * at - 1))
     store_all(send_ref, stage)
 
 
@@ -68,8 +69,8 @@
     backwards = jnp.where(row_ids + col_ids == LANES - 1, 1.0, 0.0).astype(BF16)
     shifted[:, peers:, :] = jnp.zeros((2, peers, piece), F32)
     for e in range(per_peer):
-        g_blocks = take(stage, e, peers, ROWS_OUT, (0, 1))
-        u_blocks = take(stage, per_peer + e, peers, ROWS_OUT, (0, 1))
+        g_blocks = take(stage, e, peers, OWN, (0, 1))
+        u_blocks = take(stage, e, peers, OWN, (2, 3))
         shifted[0, 0:peers, :] = g_blocks
         shifted[1, 0:peers, 0:LANES] = g_blocks[:, LANES:]
         shifted[1, 0:peers, LANES:] = shifted[0, batch : peers + batch, 0:LANES]
@@ -78,10 +79,9 @@
                 hankel[half * peers : (half + 1) * peers, step * piece : (step + 1) * piece] = shifted[
                     half, batch * step : batch * step + peers, :
                 ].astype(BF16)
-        first = per_peer * ROWS_OUT
         halves = [
-            take(stage, e * ROWS_OUT + half, pieces, first, (2,))
-            + take(stage, e * ROWS_OUT + 2 + half, pieces, first, (2,))
+            take(stage, e * OWN + half, pieces, batch * OWN, (4,))
+            + take(stage, e * OWN + 2 + half, pieces, batch * OWN, (4,))
             for half in range(2)
         ]
         before = jnp.zeros((LANES, LANES), F32)
@@ -100,7 +100,7 @@
         conv = both[:, 0:LANES] + both[:, LANES:]
         conv = jnp.concatenate([conv[0:peers], conv[peers:]], axis=1)
         gain = skip_ref[e * peers + place]
-        put(out, e, ROWS_BACK, conv + gain * g_blocks, (0, 1))
+        put(out, e, OWN, conv + gain * g_blocks, (0, 1))
         u_stack = jnp.concatenate([u_blocks[:, 0:LANES], u_blocks[:, LANES:]], axis=0).astype(BF16)
         u_turned = lax.dot_general(
             backwards, u_stack, (((1,), (1,)), ((), ())), preferred_element_type=F32
@@ -117,25 +117,21 @@
             kgrad[place_in : place_in + 1, half * LANES : (half + 1) * LANES] = lags
     lags = kgrad[...]
     high = lags.astype(BF16).astype(F32)
-    put(out, per_peer, ROWS_BACK, high, (0, 1))
-    put(out, per_peer + 1, ROWS_BACK, lags - high, (0, 1))
-    for row in range(per_peer + 2, ROWS_BACK):
-        put(out, row, ROWS_BACK, jnp.zeros((peers, piece), F32), (0, 1))
+    for part, values in enumerate((high, lags - high)):
+        for half in range(2):
+            put(out, 2 * part + half, OWN, values[:, half * LANES : (half + 1) * LANES], (2,))
     store_all(back_ref, out)
 
 
 def unpack_kernel(recv_ref, grad_inputs_ref, grad_kernel_ref, stage):
     peers = recv_ref.shape[0]
-    per_peer = grad_inputs_ref.shape[1] // peers
     load_all(stage, recv_ref)
-    rows = jnp.concatenate(
-        [take(stage, e, peers, ROWS_BACK, (0, 1)) for e in range(per_peer)], axis=0
-    )
+    rows = jnp.concatenate([take(stage, e, peers, OWN, (0, 1)) for e in range(OWN)], axis=0)
     grad_inputs_ref[...] = rows.T.astype(BF16)
-    lags = take(stage, per_peer, peers, ROWS_BACK, (0, 1)) + take(
-        stage, per_peer + 1, peers, ROWS_BACK, (0, 1)
-    )
-    grad_kernel_ref[...] = lags.T
+    for half in range(2):
+        grad_kernel_ref[:, half * LANES : (half + 1) * LANES] = take(
+            stage, half, peers, OWN, (2,)
+        ) + take(stage, 2 + half, peers, OWN, (2,))
 
 
 def shards(inputs, grad_out, kernel, skip):
@@ -143,29 +139,40 @@
     _, piece, channels = inputs.shape
     vmem = pl.BlockSpec(memory_space=pltpu.VMEM)
     smem = pl.BlockSpec(memory_space=pltpu.SMEM)
+    hbm = pl.BlockSpec(memory_space=pltpu.HBM)
     params = pltpu.CompilerParams(vmem_limit_bytes=40 * 2**20)
+    fetching = pltpu.CompilerParams(vmem_limit_bytes=60 * 2**20)
+    kernel_rows = kernel.T
+    stage_out = pltpu.VMEM((5, peers * OWN, LANES), F32)
+    stage_back = pltpu.VMEM((3, peers * OWN, LANES), F32)
     send = pl.pallas_call(
         pack_kernel,
-        out_shape=jax.ShapeDtypeStruct((peers, ROWS_OUT, piece + LANES), BF16),
-        in_specs=[vmem] * 3,
+        out_shape=jax.ShapeDtypeStruct((peers, OWN, 5 * LANES), BF16),
+        in_specs=[hbm] * 3,
         out_specs=vmem,
-        scratch_shapes=[pltpu.VMEM((3, peers * ROWS_OUT, LANES), F32)],
-        compiler_params=params,
-    )(inputs[0], grad_out[0], kernel)
+        scratch_shapes=[
+            pltpu.VMEM((piece, channels), BF16),
+            pltpu.VMEM((piece, channels), BF16),
+            pltpu.VMEM(kernel_rows.shape, F32),
+            stage_out,
+            pltpu.SemaphoreType.DMA((3,)),
+        ],
+        compiler_params=fetching,
+    )(inputs[0], grad_out[0], kernel_rows)
     recv = lax.all_to_all(send, GROUP, 0, 0, tiled=True)
     place = lax.axis_index(GROUP).astype(jnp.int32).reshape(1)
     back = pl.pallas_call(
         correlate_kernel,
-        out_shape=jax.ShapeDtypeStruct((peers, ROWS_BACK, piece), BF16),
+        out_shape=jax.ShapeDtypeStruct((peers, OWN, 3 * LANES), BF16),
         in_specs=[smem, smem, vmem],
         out_specs=vmem,
         scratch_shapes=[
-            pltpu.VMEM((3, peers * ROWS_OUT, LANES), F32),
+            stage_out,
             pltpu.VMEM((2, 2 * peers, piece), F32),
             pltpu.VMEM((2 * peers, 4096), BF16),
             pltpu.VMEM((2 * LANES, 4096), BF16),
             pltpu.VMEM((peers, piece), F32),
-            pltpu.VMEM((2, peers * ROWS_BACK, LANES), F32),
+            stage_back,
         ],
         compiler_params=params,
     )(place, skip, recv)
@@ -174,14 +181,14 @@
         unpack_kernel,
         out_shape=(
             jax.ShapeDtypeStruct((piece, channels), BF16),
-            jax.ShapeDtypeStruct(kernel.shape, F32),
+            jax.ShapeDtypeStruct(kernel_rows.shape, F32),
         ),
         in_specs=[vmem],
         out_specs=(vmem, vmem),
-        scratch_shapes=[pltpu.VMEM((2, peers * ROWS_BACK, LANES), F32)],
+        scratch_shapes=[stage_back],
         compiler_params=params,
     )(landed)
-    return (grad_inputs[None], grad_kernel)
+    return (grad_inputs[None], grad_kernel.T)
 
 
 def solution(mesh):

time: 55.1 us -> 50.9 us (0.924)
  local copies, waits for them, and re-layouts: 2.59 us -> 0.01 us
  waiting for transfers between devices: 14.5 us -> 13.1 us
  blocking collectives: 16.9 us -> 15.8 us
  Pallas kernels: 8.12 us -> 9.1 us
    unnamed x8 -> x2, local copies, waits for them, and re-layouts: 2.59 us -> 0.01 us
    all_to_all x1, waiting for transfers between devices: 14.5 us -> 13.1 us  [shards(): recv = lax.all_to_all(send, GROUP, 0, 0, tiled=True)]
    all_to_all x1, blocking collectives: 16.9 us -> 15.8 us  [shards(): landed = lax.all_to_all(back, GROUP, 0, 0, tiled=True)]
    pallas_call x2, Pallas kernels: 7.32 us -> 8.29 us  [the longest x1 6.33 us: shards(): pl.pallas_call(correlate_kernel, out_shape=jax.ShapeDtypeStruct((peers, O...]
where the time goes in v1:
time: 50.9 us; the launch traced here: 50.4 us
  blocking collectives  15.8 us (31%)
  waiting for transfers between devices  13.1 us (26%)
  starting transfers between devices  11.7 us (23%)
  Pallas kernels  9.1 us (18%)
  between operations  0.67 us (1%)
    all_to_all x1, blocking collectives, shards(): landed = lax.all_to_all(back, GROUP, 0, 0, tiled=True)  15.8 us
    all_to_all x1, waiting for transfers between devices, shards(): recv = lax.all_to_all(send, GROUP, 0, 0, tiled=True)  13.1 us
    all_to_all x1, starting transfers between devices, shards(): recv = lax.all_to_all(send, GROUP, 0, 0, tiled=True)  11.7 us
    pallas_call x1, Pallas kernels, shards(): pl.pallas_call(correlate_kernel, out_shape=jax.ShapeDtypeStruct((peers, O...  6.33 us
    pallas_call x1, Pallas kernels, shards(): pl.pallas_call(pack_kernel, out_shape=jax.ShapeDtypeStruct((peers, OWN, 5...  1.96 us
  transfers between devices with their start and end apart: 1, of which 1 were waited for; matrix products, arithmetic and copies ran while one was open for 0% of the time, Pallas kernels for 0%

profile of v1, /device:TPU:32, one launch (start us, length us, event | category | flops | bytes accessed | tf_op | source)
XLA Modules:
  0.0 50.4 jit_solution(7070432243300791868)
XLA Ops:
  0.6 2.0 %shard_map.59 = bf16[64,4,640]{2,1,0:T(4,128)(2,1)} custom-call(bf16[256,256]{1,0:T(8,128)(2,1)} %bitcast.6, bf16[256,256]{1,0:T(8,128)(2,1)} %bitcast.7, f32[64,256]{1,0:T(8,128)} %bitcast.8), custom_call_target="tpu_custom_call" | custom-call | tf_op jit(solution)/shard_map/pallas_call | solution.py:148
  2.6 11.7 %all-to-all-start = ((bf16[64,4,640]{2,1,0:T(4,128)(2,1)}), bf16[64,4,640]{2,1,0:T(4,128)(2,1)S(1)}, u32[]{:S(2)}, u32[]{:S(2)}) async-start(bf16[64,4,640]{2,1,0:T(4,128)(2,1)} %shard_map.59), calls=%async_computation | async-start | bytes 655360 | tf_op jit(solution)/shard_map/all_to_all | solution.py:162
  14.3 0.0 copy-start
  14.3 13.1 %all-to-all-done.recv_ref = bf16[64,4,640]{2,1,0:T(4,128)(2,1)S(1)} async-done(((bf16[64,4,640]{2,1,0:T(4,128)(2,1)}), bf16[64,4,640]{2,1,0:T(4,128)(2,1)S(1)}, u32[]{:S(2)}, u32[]{:S(2)}) %all-to-all-start) | async-done | bytes 327712 | tf_op jit(solution)/shard_map/all_to_all | solution.py:162
  27.4 0.0 copy-done
  27.4 6.3 %shard_map.60 = bf16[64,4,384]{2,1,0:T(4,128)(2,1)S(1)} custom-call(s32[1]{0:T(128)} %bitcast.place_ref, f32[256]{0:T(256)S(1)} %copy-done, bf16[64,4,640]{2,1,0:T(4,128)(2,1)S(1)} %all-to-all-done.recv_ref), custom_call_target="tpu_custom_call" | custom-call | tf_op jit(solution)/shard_map/pallas_call | solution.py:164
  33.8 15.8 %all_to_all.10.recv_ref = bf16[64,4,384]{2,1,0:T(4,128)(2,1)S(1)} all-to-all(bf16[64,4,384]{2,1,0:T(4,128)(2,1)S(1)} %shard_map.60), channel_id=1, replica_groups=mesh['seq'=16,'chan'=4,'dp'=4] {'seq','dp'}, dimensions={0} | all-to-all | bytes 393216 | tf_op jit(solution)/shard_map/all_to_all | solution.py:179
  49.6 0.8 %shard_map.61 = (bf16[256,256]{1,0:T(8,128)(2,1)}, f32[64,256]{1,0:T(8,128)}) custom-call(bf16[64,4,384]{2,1,0:T(4,128)(2,1)S(1)} %all_to_all.10.recv_ref), custom_call_target="tpu_custom_call" | custom-call | tf_op jit(solution)/shard_map/pallas_call | solution.py:180
Async XLA Ops:
  2.6 24.8 %all-to-all-start = ((bf16[64,4,640]{2,1,0:T(4,128)(2,1)}), bf16[64,4,640]{2,1,0:T(4,128)(2,1)S(1)}, u32[]{:S(2)}, u32[]{:S(2)}) async-start(bf16[64,4,640]{2,1,0:T(4,128)(2,1)} %shard_map.59), calls=%async_computation | async-start | bytes 655360 | tf_op jit(solution)/shard_map/all_to_all | solution.py:162
  14.3 13.2 %copy-start = (f32[256]{0:T(256)S(1)}, f32[256]{0:T(256)}, u32[]{:S(2)}) copy-start(f32[256]{0:T(256)} %skip_ref.1) | copy-start | bytes 3076

commit v2 on v1

--- a/solution.py
+++ b/solution.py
@@ -7,9 +7,12 @@
 
 F32 = jnp.float32
 BF16 = jnp.bfloat16
-GROUP = ("seq", "dp")
+MESH_AXES = ("seq", "chan", "dp")
 LANES = 128
 OWN = 4
+PIECES = 16
+BATCH = 4
+CHUNK = 4
 
 
 def take(stage, first, count, stride, blocks):
@@ -56,70 +59,100 @@
     store_all(send_ref, stage)
 
 
-def correlate_kernel(place_ref, skip_ref, recv_ref, back_ref, stage, shifted, hankel, toeplitz, kgrad, out):
+def rows_of(b):
+    return (b % 2) * 2 * PIECES + b // 2, 2
+
+
+def correlate_kernel(place_ref, skip_ref, recv_ref, back_ref, stage, blocks, result, hankels, toeplitz, partial_rows, out):
     peers = recv_ref.shape[0]
-    pieces, piece, per_peer = 16, 256, 4
-    batch = peers // pieces
     place = place_ref[0]
+    piece = 2 * LANES
     load_all(stage, recv_ref)
     row_ids = lax.broadcasted_iota(jnp.int32, (LANES, LANES), 0)
     col_ids = lax.broadcasted_iota(jnp.int32, (LANES, LANES), 1)
-    on_or_after = col_ids >= row_ids
     after = col_ids > row_ids
     backwards = jnp.where(row_ids + col_ids == LANES - 1, 1.0, 0.0).astype(BF16)
-    shifted[:, peers:, :] = jnp.zeros((2, peers, piece), F32)
-    for e in range(per_peer):
-        g_blocks = take(stage, e, peers, OWN, (0, 1))
-        u_blocks = take(stage, e, peers, OWN, (2, 3))
-        shifted[0, 0:peers, :] = g_blocks
-        shifted[1, 0:peers, 0:LANES] = g_blocks[:, LANES:]
-        shifted[1, 0:peers, LANES:] = shifted[0, batch : peers + batch, 0:LANES]
-        for step in range(pieces):
-            for half in range(2):
-                hankel[half * peers : (half + 1) * peers, step * piece : (step + 1) * piece] = shifted[
-                    half, batch * step : batch * step + peers, :
-                ].astype(BF16)
+    turn = jnp.where((row_ids + col_ids) % LANES == 0, 1.0, 0.0).astype(BF16)
+    stage[4] = jnp.dot(stage[4].astype(BF16), turn, preferred_element_type=F32)
+    for e in range(OWN):
+        for half in range(2):
+            blocks[e, half, peers:, :] = jnp.zeros((peers + 8, LANES), F32)
+            for kind in range(2):
+                for b in range(BATCH):
+                    first, step = rows_of(b)
+                    values = stage[2 * kind + half, pl.ds(first * OWN + e, PIECES, stride=step * OWN), :]
+                    blocks[e, 2 * kind + half, pl.ds(b, PIECES, stride=BATCH), :] = values
+        k_first, k_step = rows_of(e)
         halves = [
-            take(stage, e * OWN + half, pieces, batch * OWN, (4,))
-            + take(stage, e * OWN + 2 + half, pieces, batch * OWN, (4,))
+            stage[4, pl.ds(k_first * OWN + half, PIECES, stride=k_step * OWN), :]
+            + stage[4, pl.ds(k_first * OWN + 2 + half, PIECES, stride=k_step * OWN), :]
             for half in range(2)
         ]
-        before = jnp.zeros((LANES, LANES), F32)
-        for block in range(2 * pieces):
+
+        def later_blocks(half, lag):
+            return blocks[e, half, BATCH * lag : BATCH * lag + peers, :].astype(BF16)
+
+        def toeplitz_rows(block, before):
             values = halves[block % 2][block // 2 : block // 2 + 1, :]
             turned = pltpu.roll(jnp.broadcast_to(values, (LANES, LANES)), 0, 1, stride=1, stride_axis=0)
-            square = jnp.where(on_or_after, turned, before)
-            before = turned
+            square = jnp.where(col_ids <= row_ids, turned, before)
             high = square.astype(BF16)
-            columns = slice(block * LANES, (block + 1) * LANES)
-            toeplitz[0:LANES, columns] = high
-            toeplitz[LANES:, columns] = (square - high.astype(F32)).astype(BF16)
-        both = lax.dot_general(
-            hankel[...], toeplitz[...], (((1,), (1,)), ((), ())), preferred_element_type=F32
-        )
-        conv = both[:, 0:LANES] + both[:, LANES:]
-        conv = jnp.concatenate([conv[0:peers], conv[peers:]], axis=1)
-        gain = skip_ref[e * peers + place]
-        put(out, e, OWN, conv + gain * g_blocks, (0, 1))
-        u_stack = jnp.concatenate([u_blocks[:, 0:LANES], u_blocks[:, LANES:]], axis=0).astype(BF16)
+            return jnp.concatenate([high, (square - high.astype(F32)).astype(BF16)], axis=1), turned
+
+        def add_diagonals(block, turned, earlier):
+            chosen = jnp.where(after, turned, earlier)
+            partial_rows[e, 8 * block : 8 * block + 8, :] = jnp.sum(chosen.reshape(LANES // 8, 8, LANES), axis=0)
+
+        u_stack = jnp.concatenate([blocks[e, 2, 0:peers, :], blocks[e, 3, 0:peers, :]], axis=0).astype(BF16)
         u_turned = lax.dot_general(
             backwards, u_stack, (((1,), (1,)), ((), ())), preferred_element_type=F32
         ).astype(BF16)
-        later = jnp.zeros((LANES, LANES), F32)
-        for block in range(2 * pieces - 1, -1, -1):
-            columns = slice(block * LANES, (block + 1) * LANES)
-            products = jnp.dot(u_turned, hankel[:, columns], preferred_element_type=F32)
-            turned = pltpu.roll(products, 1, 1, stride=1, stride_axis=0)
-            lags = jnp.sum(jnp.where(after, later, turned), axis=0, keepdims=True)
-            later = turned
-            place_in = (block // 2) * per_peer + e
-            half = block % 2
-            kgrad[place_in : place_in + 1, half * LANES : (half + 1) * LANES] = lags
-    lags = kgrad[...]
-    high = lags.astype(BF16).astype(F32)
-    for part, values in enumerate((high, lags - high)):
-        for half in range(2):
-            put(out, 2 * part + half, OWN, values[:, half * LANES : (half + 1) * LANES], (2,))
+        before = jnp.zeros((LANES, LANES), F32)
+        even = later_blocks(0, 0)
+        earlier = None
+        both = None
+        for step in range(PIECES):
+            odd, following = later_blocks(1, step), later_blocks(0, step + 1)
+            hankel = jnp.concatenate(
+                [jnp.concatenate([even, odd], axis=1), jnp.concatenate([odd, following], axis=1)], axis=0
+            )
+            even = following
+            first_rows, before = toeplitz_rows(2 * step, before)
+            last_rows, before = toeplitz_rows(2 * step + 1, before)
+            columns = slice(step * piece, (step + 1) * piece)
+            hankels[e, :, columns] = hankel
+            toeplitz[e, 2 * step * LANES : (2 * step + 1) * LANES, :] = first_rows
+            toeplitz[e, (2 * step + 1) * LANES : (2 * step + 2) * LANES, :] = last_rows
+            if (step + 1) % CHUNK == 0:
+                chunk = slice((step + 1 - CHUNK) * piece, (step + 1) * piece)
+                added = jnp.dot(hankels[e, :, chunk], toeplitz[e, chunk, :], preferred_element_type=F32)
+                both = added if both is None else both + added
+            products = jnp.dot(u_turned, hankel, preferred_element_type=F32)
+            for half in range(2):
+                turned = pltpu.roll(
+                    products[:, half * LANES : (half + 1) * LANES], 1, 1, stride=1, stride_axis=0
+                )
+                if earlier is not None:
+                    add_diagonals(2 * step + half - 1, turned, earlier)
+                earlier = turned
+        add_diagonals(2 * PIECES - 1, jnp.zeros_like(earlier), earlier)
+        for half in range(2):
+            lags = sum(
+                partial_rows[e, pl.ds(8 * half + row, PIECES, stride=16), :] for row in range(8)
+            )
+            high = lags.astype(BF16).astype(F32)
+            for part, values in enumerate((high, lags - high)):
+                first = k_first * OWN + 2 * part + half
+                out[2, pl.ds(first, PIECES, stride=k_step * OWN), :] = values
+        conv = both[:, 0:LANES] + both[:, LANES:]
+        gain = skip_ref[e * peers + place]
+        for half in range(2):
+            result[e, half] = conv[half * peers : (half + 1) * peers] + gain * blocks[e, half, 0:peers, :]
+            for b in range(BATCH):
+                first, step = rows_of(b)
+                out[half, pl.ds(first * OWN + e, PIECES, stride=step * OWN), :] = result[
+                    e, half, pl.ds(b, PIECES, stride=BATCH), :
+                ]
     store_all(back_ref, out)
 
 
@@ -134,8 +167,21 @@
         ) + take(stage, 2 + half, peers, OWN, (2,))
 
 
+def exchange(blocks):
+    chans = lax.axis_size("chan")
+    groups = []
+    for chan in range(chans):
+        group = [0] * (PIECES * BATCH)
+        for b in range(BATCH):
+            first, step = rows_of(b)
+            for piece in range(PIECES):
+                group[first + step * piece] = (piece * chans + chan) * BATCH + b
+        groups.append(group)
+    return lax.all_to_all(blocks, MESH_AXES, 0, 0, axis_index_groups=groups, tiled=True)
+
+
 def shards(inputs, grad_out, kernel, skip):
-    peers = lax.axis_size(GROUP)
+    peers = PIECES * BATCH
     _, piece, channels = inputs.shape
     vmem = pl.BlockSpec(memory_space=pltpu.VMEM)
     smem = pl.BlockSpec(memory_space=pltpu.SMEM)
@@ -159,8 +205,9 @@
         ],
         compiler_params=fetching,
     )(inputs[0], grad_out[0], kernel_rows)
-    recv = lax.all_to_all(send, GROUP, 0, 0, tiled=True)
-    place = lax.axis_index(GROUP).astype(jnp.int32).reshape(1)
+    recv = exchange(send)
+    b, piece_id = lax.axis_index("dp"), lax.axis_index("seq")
+    place = ((b % 2) * 2 * PIECES + b // 2 + 2 * piece_id).astype(jnp.int32).reshape(1)
     back = pl.pallas_call(
         correlate_kernel,
         out_shape=jax.ShapeDtypeStruct((peers, OWN, 3 * LANES), BF16),
@@ -168,15 +215,16 @@
         out_specs=vmem,
         scratch_shapes=[
             stage_out,
-            pltpu.VMEM((2, 2 * peers, piece), F32),
-            pltpu.VMEM((2 * peers, 4096), BF16),
-            pltpu.VMEM((2 * LANES, 4096), BF16),
-            pltpu.VMEM((peers, piece), F32),
+            pltpu.VMEM((OWN, 4, 2 * peers + 8, LANES), F32),
+            pltpu.VMEM((OWN, 2, peers, LANES), F32),
+            pltpu.VMEM((OWN, 2 * peers, PIECES * piece), BF16),
+            pltpu.VMEM((OWN, PIECES * piece, 2 * LANES), BF16),
+            pltpu.VMEM((OWN, 16 * PIECES, LANES), F32),
             stage_back,
         ],
         compiler_params=params,
     )(place, skip, recv)
-    landed = lax.all_to_all(back, GROUP, 0, 0, tiled=True)
+    landed = exchange(back)
     grad_inputs, grad_kernel = pl.pallas_call(
         unpack_kernel,
         out_shape=(

time: 50.9 us -> 50 us (0.982)
  blocking collectives: 15.8 us -> 16.6 us
  Pallas kernels: 9.1 us -> 8.34 us
  waiting for transfers between devices: 13.1 us -> 12.4 us
    all_to_all x1, blocking collectives: 15.8 us -> 16.6 us  [exchange(): lax.all_to_all(blocks, MESH_AXES, 0, 0, axis_index_groups=groups, tiled=T...]
    pallas_call x1, Pallas kernels: 6.33 us -> 5.57 us  [shards(): pl.pallas_call(correlate_kernel, out_shape=jax.ShapeDtypeStruct((peers, O...]
    all_to_all x1, waiting for transfers between devices: 13.1 us -> 12.4 us  [exchange(): lax.all_to_all(blocks, MESH_AXES, 0, 0, axis_index_groups=groups, tiled=T...]
where the time goes in v2:
time: 50 us; the launch traced here: 49.8 us
  blocking collectives  16.6 us (33%)
  waiting for transfers between devices  12.4 us (25%)
  starting transfers between devices  11.8 us (24%)
  Pallas kernels  8.34 us (17%)
  between operations  0.68 us (1%)
    all_to_all x1, blocking collectives, exchange(): lax.all_to_all(blocks, MESH_AXES, 0, 0, axis_index_groups=groups, tiled=T...  16.6 us
    all_to_all x1, waiting for transfers between devices, exchange(): lax.all_to_all(blocks, MESH_AXES, 0, 0, axis_index_groups=groups, tiled=T...  12.4 us
    all_to_all x1, starting transfers between devices, exchange(): lax.all_to_all(blocks, MESH_AXES, 0, 0, axis_index_groups=groups, tiled=T...  11.8 us
    pallas_call x1, Pallas kernels, shards(): pl.pallas_call(correlate_kernel, out_shape=jax.ShapeDtypeStruct((peers, O...  5.57 us
    pallas_call x1, Pallas kernels, shards(): pl.pallas_call(pack_kernel, out_shape=jax.ShapeDtypeStruct((peers, OWN, 5...  1.96 us
  transfers between devices with their start and end apart: 1, of which 1 were waited for; matrix products, arithmetic and copies ran while one was open for 0% of the time, Pallas kernels for 0%

profile of v2, /device:TPU:32, one launch (start us, length us, event | category | flops | bytes accessed | tf_op | source)
XLA Modules:
  0.0 49.8 jit_solution(2827819308956587737)
XLA Ops:
  0.6 2.0 %shard_map.59 = bf16[64,4,640]{2,1,0:T(4,128)(2,1)} custom-call(bf16[256,256]{1,0:T(8,128)(2,1)} %bitcast.6, bf16[256,256]{1,0:T(8,128)(2,1)} %bitcast.7, f32[64,256]{1,0:T(8,128)} %bitcast.8), custom_call_target="tpu_custom_call" | custom-call | tf_op jit(solution)/shard_map/pallas_call | solution.py:194
  2.6 11.8 %all-to-all-start = ((bf16[64,4,640]{2,1,0:T(4,128)(2,1)}), bf16[64,4,640]{2,1,0:T(4,128)(2,1)S(1)}, u32[]{:S(2)}, u32[]{:S(2)}) async-start(bf16[64,4,640]{2,1,0:T(4,128)(2,1)} %shard_map.59), calls=%async_computation | async-start | bytes 655360 | tf_op jit(solution)/shard_map/all_to_all | solution.py:180
  14.4 0.0 copy-start
  14.4 12.4 %all-to-all-done.recv_ref = bf16[64,4,640]{2,1,0:T(4,128)(2,1)S(1)} async-done(((bf16[64,4,640]{2,1,0:T(4,128)(2,1)}), bf16[64,4,640]{2,1,0:T(4,128)(2,1)S(1)}, u32[]{:S(2)}, u32[]{:S(2)}) %all-to-all-start) | async-done | bytes 327712 | tf_op jit(solution)/shard_map/all_to_all | solution.py:180
  26.8 0.0 copy-done
  26.8 5.6 %shard_map.60 = bf16[64,4,384]{2,1,0:T(4,128)(2,1)S(1)} custom-call(s32[1]{0:T(128)} %bitcast.place_ref, f32[256]{0:T(256)S(1)} %copy-done, bf16[64,4,640]{2,1,0:T(4,128)(2,1)S(1)} %all-to-all-done.recv_ref), custom_call_target="tpu_custom_call" | custom-call | tf_op jit(solution)/shard_map/pallas_call | solution.py:211
  32.4 16.6 %all_to_all.10.recv_ref = bf16[64,4,384]{2,1,0:T(4,128)(2,1)S(1)} all-to-all(bf16[64,4,384]{2,1,0:T(4,128)(2,1)S(1)} %shard_map.60), channel_id=1, replica_groups={{0,2,16,18,32,34,48,50,64,66,80,82,96,98,112,114,128,130,144,146,160,16..., dimensions={0} | all-to-all | bytes 393216 | tf_op jit(solution)/shard_map/all_to_all | solution.py:180
  49.0 0.8 %shard_map.61 = (bf16[256,256]{1,0:T(8,128)(2,1)}, f32[64,256]{1,0:T(8,128)}) custom-call(bf16[64,4,384]{2,1,0:T(4,128)(2,1)S(1)} %all_to_all.10.recv_ref), custom_call_target="tpu_custom_call" | custom-call | tf_op jit(solution)/shard_map/pallas_call | solution.py:228
Async XLA Ops:
  2.6 24.2 %all-to-all-start = ((bf16[64,4,640]{2,1,0:T(4,128)(2,1)}), bf16[64,4,640]{2,1,0:T(4,128)(2,1)S(1)}, u32[]{:S(2)}, u32[]{:S(2)}) async-start(bf16[64,4,640]{2,1,0:T(4,128)(2,1)} %shard_map.59), calls=%async_computation | async-start | bytes 655360 | tf_op jit(solution)/shard_map/all_to_all | solution.py:180
  14.4 12.4 %copy-start = (f32[256]{0:T(256)S(1)}, f32[256]{0:T(256)}, u32[]{:S(2)}) copy-start(f32[256]{0:T(256)} %skip_ref.1) | copy-start | bytes 3076

commit v3 on v2

--- a/solution.py
+++ b/solution.py
@@ -12,6 +12,7 @@
 OWN = 4
 PIECES = 16
 BATCH = 4
+BLOCK = 64
 CHUNK = 4
 
 
@@ -63,15 +64,20 @@
     return (b % 2) * 2 * PIECES + b // 2, 2
 
 
-def correlate_kernel(place_ref, skip_ref, recv_ref, back_ref, stage, blocks, result, hankels, toeplitz, partial_rows, out):
+def correlate_kernel(skip_hbm, recv_ref, back_ref, skip_ref, sem, stage, blocks, result, hankels, toeplitz, partial_rows, out):
     peers = recv_ref.shape[0]
-    place = place_ref[0]
+    fetch = pltpu.make_async_copy(skip_hbm, skip_ref, sem)
+    fetch.start()
+    first, step = rows_of(lax.axis_index("dp"))
+    place = first + step * lax.axis_index("seq")
     piece = 2 * LANES
     load_all(stage, recv_ref)
     row_ids = lax.broadcasted_iota(jnp.int32, (LANES, LANES), 0)
     col_ids = lax.broadcasted_iota(jnp.int32, (LANES, LANES), 1)
-    after = col_ids > row_ids
-    backwards = jnp.where(row_ids + col_ids == LANES - 1, 1.0, 0.0).astype(BF16)
+    after = col_ids[0:BLOCK] > row_ids[0:BLOCK] + BLOCK
+    flip_rows = lax.broadcasted_iota(jnp.int32, (piece, piece), 0)
+    flip_cols = lax.broadcasted_iota(jnp.int32, (piece, piece), 1)
+    flip = jnp.where(flip_cols == flip_rows + (BLOCK - 1) - 2 * (flip_rows % BLOCK), 1.0, 0.0).astype(BF16)
     turn = jnp.where((row_ids + col_ids) % LANES == 0, 1.0, 0.0).astype(BF16)
     stage[4] = jnp.dot(stage[4].astype(BF16), turn, preferred_element_type=F32)
     for e in range(OWN):
@@ -101,26 +107,39 @@
 
         def add_diagonals(block, turned, earlier):
             chosen = jnp.where(after, turned, earlier)
-            partial_rows[e, 8 * block : 8 * block + 8, :] = jnp.sum(chosen.reshape(LANES // 8, 8, LANES), axis=0)
-
-        u_stack = jnp.concatenate([blocks[e, 2, 0:peers, :], blocks[e, 3, 0:peers, :]], axis=0).astype(BF16)
-        u_turned = lax.dot_general(
-            backwards, u_stack, (((1,), (1,)), ((), ())), preferred_element_type=F32
+            partial_rows[e, 8 * block : 8 * block + 8, :] = jnp.sum(chosen.reshape(BLOCK // 8, 8, LANES), axis=0)
+
+        left, right = blocks[e, 0, 0:peers, :], blocks[e, 1, 0:peers, :]
+        following = blocks[e, 0, BATCH : peers + BATCH, :]
+        blocks[e, 4, 0:peers, :] = jnp.concatenate([left[:, BLOCK:], right[:, :BLOCK]], axis=1)
+        blocks[e, 5, 0:peers, :] = jnp.concatenate([right[:, BLOCK:], following[:, :BLOCK]], axis=1)
+        for half in range(2):
+            blocks[e, 4 + half, peers:, :] = jnp.zeros((peers + 8, LANES), F32)
+        u_rows = jnp.concatenate([blocks[e, 2, 0:peers, :], blocks[e, 3, 0:peers, :]], axis=1).astype(BF16)
+        u_turned = lax.dot_general(flip, u_rows, (((1,), (1,)), ((), ())), preferred_element_type=F32)
+        u_turned = jnp.concatenate(
+            [u_turned[at * BLOCK : (at + 1) * BLOCK] for at in (0, 2, 1, 3)], axis=1
         ).astype(BF16)
         before = jnp.zeros((LANES, LANES), F32)
-        even = later_blocks(0, 0)
+        now = [later_blocks(at, 0) for at in (0, 4)]
         earlier = None
         both = None
         for step in range(PIECES):
-            odd, following = later_blocks(1, step), later_blocks(0, step + 1)
+            odd = [later_blocks(at, step) for at in (1, 5)]
+            following = [later_blocks(at, step + 1) for at in (0, 4)]
             hankel = jnp.concatenate(
-                [jnp.concatenate([even, odd], axis=1), jnp.concatenate([odd, following], axis=1)], axis=0
+                [
+                    jnp.concatenate(pair, axis=1)
+                    for at in range(2)
+                    for pair in ((now[at], odd[at]), (odd[at], following[at]))
+                ],
+                axis=0,
             )
-            even = following
+            now = following
             first_rows, before = toeplitz_rows(2 * step, before)
             last_rows, before = toeplitz_rows(2 * step + 1, before)
             columns = slice(step * piece, (step + 1) * piece)
-            hankels[e, :, columns] = hankel
+            hankels[e, :, columns] = hankel[0 : 2 * peers]
             toeplitz[e, 2 * step * LANES : (2 * step + 1) * LANES, :] = first_rows
             toeplitz[e, (2 * step + 1) * LANES : (2 * step + 2) * LANES, :] = last_rows
             if (step + 1) % CHUNK == 0:
@@ -130,7 +149,7 @@
             products = jnp.dot(u_turned, hankel, preferred_element_type=F32)
             for half in range(2):
                 turned = pltpu.roll(
-                    products[:, half * LANES : (half + 1) * LANES], 1, 1, stride=1, stride_axis=0
+                    products[:, half * LANES : (half + 1) * LANES], BLOCK + 1, 1, stride=1, stride_axis=0
                 )
                 if earlier is not None:
                     add_diagonals(2 * step + half - 1, turned, earlier)
@@ -145,6 +164,8 @@
                 first = k_first * OWN + 2 * part + half
                 out[2, pl.ds(first, PIECES, stride=k_step * OWN), :] = values
         conv = both[:, 0:LANES] + both[:, LANES:]
+        if e == 0:
+            fetch.wait()
         gain = skip_ref[e * peers + place]
         for half in range(2):
             result[e, half] = conv[half * peers : (half + 1) * peers] + gain * blocks[e, half, 0:peers, :]
@@ -184,7 +205,6 @@
     peers = PIECES * BATCH
     _, piece, channels = inputs.shape
     vmem = pl.BlockSpec(memory_space=pltpu.VMEM)
-    smem = pl.BlockSpec(memory_space=pltpu.SMEM)
     hbm = pl.BlockSpec(memory_space=pltpu.HBM)
     params = pltpu.CompilerParams(vmem_limit_bytes=40 * 2**20)
     fetching = pltpu.CompilerParams(vmem_limit_bytes=60 * 2**20)
@@ -206,16 +226,16 @@
         compiler_params=fetching,
     )(inputs[0], grad_out[0], kernel_rows)
     recv = exchange(send)
-    b, piece_id = lax.axis_index("dp"), lax.axis_index("seq")
-    place = ((b % 2) * 2 * PIECES + b // 2 + 2 * piece_id).astype(jnp.int32).reshape(1)
     back = pl.pallas_call(
         correlate_kernel,
         out_shape=jax.ShapeDtypeStruct((peers, OWN, 3 * LANES), BF16),
-        in_specs=[smem, smem, vmem],
+        in_specs=[hbm, vmem],
         out_specs=vmem,
         scratch_shapes=[
+            pltpu.SMEM(skip.shape, F32),
+            pltpu.SemaphoreType.DMA(()),
             stage_out,
-            pltpu.VMEM((OWN, 4, 2 * peers + 8, LANES), F32),
+            pltpu.VMEM((OWN, 6, 2 * peers + 8, LANES), F32),
             pltpu.VMEM((OWN, 2, peers, LANES), F32),
             pltpu.VMEM((OWN, 2 * peers, PIECES * piece), BF16),
             pltpu.VMEM((OWN, PIECES * piece, 2 * LANES), BF16),
@@ -223,7 +243,7 @@
             stage_back,
         ],
         compiler_params=params,
-    )(place, skip, recv)
+    )(skip, recv)
     landed = exchange(back)
     grad_inputs, grad_kernel = pl.pallas_call(
         unpack_kernel,

time: 50 us -> 49.4 us (0.988)
  blocking collectives: 16.6 us -> 40.8 us
  waiting for transfers between devices: 12.4 us -> 0 us
  starting transfers between devices: 11.8 us -> 0 us
  Pallas kernels: 8.34 us -> 7.81 us
    all_to_all x1 -> x2, blocking collectives: 16.6 us -> 40.8 us  [exchange(): lax.all_to_all(blocks, MESH_AXES, 0, 0, axis_index_groups=groups, tiled=T...]
    all_to_all x1 -> x0, waiting for transfers between devices: 12.4 us -> none  [exchange(): lax.all_to_all(blocks, MESH_AXES, 0, 0, axis_index_groups=groups, tiled=T...]
    all_to_all x1 -> x0, starting transfers between devices: 11.8 us -> none  [exchange(): lax.all_to_all(blocks, MESH_AXES, 0, 0, axis_index_groups=groups, tiled=T...]
    pallas_call x1, Pallas kernels: 5.57 us -> 5.04 us  [shards(): pl.pallas_call(correlate_kernel, out_shape=jax.ShapeDtypeStruct((peers, O...]
  transfers between devices with their start and end apart: 1 -> 0, of which waited for: 1 -> 0; matrix products, arithmetic and copies ran while one was open for 0% -> 0% of each run, Pallas kernels for 0% -> 0%
where the time goes in v3:
time: 49.4 us; the launch traced here: 49.2 us
  blocking collectives  40.8 us (83%)
  Pallas kernels  7.81 us (16%)
  between operations  0.66 us (1%)
    all_to_all x2, blocking collectives, exchange(): lax.all_to_all(blocks, MESH_AXES, 0, 0, axis_index_groups=groups, tiled=T...  40.8 us
    pallas_call x1, Pallas kernels, shards(): pl.pallas_call(correlate_kernel, out_shape=jax.ShapeDtypeStruct((peers, O...  5.04 us
    pallas_call x1, Pallas kernels, shards(): pl.pallas_call(pack_kernel, out_shape=jax.ShapeDtypeStruct((peers, OWN, 5...  1.96 us

profile of v3, /device:TPU:32, one launch (start us, length us, event | category | flops | bytes accessed | tf_op | source)
XLA Modules:
  0.0 49.2 jit_solution(7231661227913282572)
XLA Ops:
  0.6 2.0 %shard_map.59 = bf16[64,4,640]{2,1,0:T(4,128)(2,1)} custom-call(bf16[256,256]{1,0:T(8,128)(2,1)} %bitcast.5, bf16[256,256]{1,0:T(8,128)(2,1)} %bitcast.6, f32[64,256]{1,0:T(8,128)} %bitcast.7), custom_call_target="tpu_custom_call" | custom-call | tf_op jit(solution)/shard_map/pallas_call | solution.py:214
  2.6 0.0 copy-start
  2.6 24.2 %all_to_all.10.recv_ref = bf16[64,4,640]{2,1,0:T(4,128)(2,1)S(1)} all-to-all(bf16[64,4,640]{2,1,0:T(4,128)(2,1)} %shard_map.59), channel_id=1, replica_groups={{0,2,16,18,32,34,48,50,64,66,80,82,96,98,112,114,128,130,144,146,160,16..., dimensions={0} | all-to-all | bytes 655360 | tf_op jit(solution)/shard_map/all_to_all | solution.py:201
  26.8 0.0 copy-done
  26.8 5.0 %shard_map.60 = bf16[64,4,384]{2,1,0:T(4,128)(2,1)S(1)} custom-call(f32[256]{0:T(256)S(1)} %copy-done, bf16[64,4,640]{2,1,0:T(4,128)(2,1)S(1)} %all_to_all.10.recv_ref), custom_call_target="tpu_custom_call" | custom-call | tf_op jit(solution)/shard_map/pallas_call | solution.py:229
  31.9 16.6 %all_to_all.11.recv_ref = bf16[64,4,384]{2,1,0:T(4,128)(2,1)S(1)} all-to-all(bf16[64,4,384]{2,1,0:T(4,128)(2,1)S(1)} %shard_map.60), channel_id=1, replica_groups={{0,2,16,18,32,34,48,50,64,66,80,82,96,98,112,114,128,130,144,146,160,16..., dimensions={0} | all-to-all | bytes 393216 | tf_op jit(solution)/shard_map/all_to_all | solution.py:201
  48.4 0.8 %shard_map.61 = (bf16[256,256]{1,0:T(8,128)(2,1)}, f32[64,256]{1,0:T(8,128)}) custom-call(bf16[64,4,384]{2,1,0:T(4,128)(2,1)S(1)} %all_to_all.11.recv_ref), custom_call_target="tpu_custom_call" | custom-call | tf_op jit(solution)/shard_map/pallas_call | solution.py:248
Async XLA Ops:
  2.6 24.2 %copy-start = (f32[256]{0:T(256)S(1)}, f32[256]{0:T(256)}, u32[]{:S(2)}) copy-start(f32[256]{0:T(256)} %skip_hbm.1) | copy-start | bytes 3076

commit v4 on v3

--- a/solution.py
+++ b/solution.py
@@ -13,7 +13,6 @@
 PIECES = 16
 BATCH = 4
 BLOCK = 64
-CHUNK = 4
 
 
 def take(stage, first, count, stride, blocks):
@@ -64,7 +63,7 @@
     return (b % 2) * 2 * PIECES + b // 2, 2
 
 
-def correlate_kernel(skip_hbm, recv_ref, back_ref, skip_ref, sem, stage, blocks, result, hankels, toeplitz, partial_rows, out):
+def correlate_kernel(skip_hbm, recv_ref, back_ref, skip_ref, sem, stage, blocks, result, partial_rows, out):
     peers = recv_ref.shape[0]
     fetch = pltpu.make_async_copy(skip_hbm, skip_ref, sem)
     fetch.start()
@@ -138,14 +137,12 @@
             now = following
             first_rows, before = toeplitz_rows(2 * step, before)
             last_rows, before = toeplitz_rows(2 * step + 1, before)
-            columns = slice(step * piece, (step + 1) * piece)
-            hankels[e, :, columns] = hankel[0 : 2 * peers]
-            toeplitz[e, 2 * step * LANES : (2 * step + 1) * LANES, :] = first_rows
-            toeplitz[e, (2 * step + 1) * LANES : (2 * step + 2) * LANES, :] = last_rows
-            if (step + 1) % CHUNK == 0:
-                chunk = slice((step + 1 - CHUNK) * piece, (step + 1) * piece)
-                added = jnp.dot(hankels[e, :, chunk], toeplitz[e, chunk, :], preferred_element_type=F32)
-                both = added if both is None else both + added
+            added = jnp.dot(
+                hankel[0 : 2 * peers],
+                jnp.concatenate([first_rows, last_rows], axis=0),
+                preferred_element_type=F32,
+            )
+            both = added if both is None else both + added
             products = jnp.dot(u_turned, hankel, preferred_element_type=F32)
             for half in range(2):
                 turned = pltpu.roll(
@@ -237,8 +234,6 @@
             stage_out,
             pltpu.VMEM((OWN, 6, 2 * peers + 8, LANES), F32),
             pltpu.VMEM((OWN, 2, peers, LANES), F32),
-            pltpu.VMEM((OWN, 2 * peers, PIECES * piece), BF16),
-            pltpu.VMEM((OWN, PIECES * piece, 2 * LANES), BF16),
             pltpu.VMEM((OWN, 16 * PIECES, LANES), F32),
             stage_back,
         ],

time: 49.4 us -> 49.3 us (level)
  no operation moved by 1% of the time
where the time goes in v4:
time: 49.3 us; the launch traced here: 49 us
  blocking collectives  40.8 us (83%)
  Pallas kernels  7.61 us (15%)
  between operations  0.66 us (1%)
    all_to_all x2, blocking collectives, exchange(): lax.all_to_all(blocks, MESH_AXES, 0, 0, axis_index_groups=groups, tiled=T...  40.8 us
    pallas_call x1, Pallas kernels, shards(): pl.pallas_call(correlate_kernel, out_shape=jax.ShapeDtypeStruct((peers, O...  4.84 us
    pallas_call x1, Pallas kernels, shards(): pl.pallas_call(pack_kernel, out_shape=jax.ShapeDtypeStruct((peers, OWN, 5...  1.96 us

profile of v4, /device:TPU:32, one launch (start us, length us, event | category | flops | bytes accessed | tf_op | source)
XLA Modules:
  0.0 49.0 jit_solution(6060915177046676221)
XLA Ops:
  0.6 2.0 %shard_map.59 = bf16[64,4,640]{2,1,0:T(4,128)(2,1)} custom-call(bf16[256,256]{1,0:T(8,128)(2,1)} %bitcast.5, bf16[256,256]{1,0:T(8,128)(2,1)} %bitcast.6, f32[64,256]{1,0:T(8,128)} %bitcast.7), custom_call_target="tpu_custom_call" | custom-call | tf_op jit(solution)/shard_map/pallas_call | solution.py:211
  2.6 0.0 copy-start
  2.6 24.2 %all_to_all.10.recv_ref = bf16[64,4,640]{2,1,0:T(4,128)(2,1)S(1)} all-to-all(bf16[64,4,640]{2,1,0:T(4,128)(2,1)} %shard_map.59), channel_id=1, replica_groups={{0,2,16,18,32,34,48,50,64,66,80,82,96,98,112,114,128,130,144,146,160,16..., dimensions={0} | all-to-all | bytes 655360 | tf_op jit(solution)/shard_map/all_to_all | solution.py:198
  26.8 0.0 copy-done
  26.8 4.8 %shard_map.60 = bf16[64,4,384]{2,1,0:T(4,128)(2,1)S(1)} custom-call(f32[256]{0:T(256)S(1)} %copy-done, bf16[64,4,640]{2,1,0:T(4,128)(2,1)S(1)} %all_to_all.10.recv_ref), custom_call_target="tpu_custom_call" | custom-call | tf_op jit(solution)/shard_map/pallas_call | solution.py:226
  31.7 16.6 %all_to_all.11.recv_ref = bf16[64,4,384]{2,1,0:T(4,128)(2,1)S(1)} all-to-all(bf16[64,4,384]{2,1,0:T(4,128)(2,1)S(1)} %shard_map.60), channel_id=1, replica_groups={{0,2,16,18,32,34,48,50,64,66,80,82,96,98,112,114,128,130,144,146,160,16..., dimensions={0} | all-to-all | bytes 393216 | tf_op jit(solution)/shard_map/all_to_all | solution.py:198
  48.2 0.8 %shard_map.61 = (bf16[256,256]{1,0:T(8,128)(2,1)}, f32[64,256]{1,0:T(8,128)}) custom-call(bf16[64,4,384]{2,1,0:T(4,128)(2,1)S(1)} %all_to_all.11.recv_ref), custom_call_target="tpu_custom_call" | custom-call | tf_op jit(solution)/shard_map/pallas_call | solution.py:243
Async XLA Ops:
  2.6 24.2 %copy-start = (f32[256]{0:T(256)S(1)}, f32[256]{0:T(256)}, u32[]{:S(2)}) copy-start(f32[256]{0:T(256)} %skip_hbm.1) | copy-start | bytes 3076

commit v5 on v4

--- a/solution.py
+++ b/solution.py
@@ -60,7 +60,7 @@
 
 
 def rows_of(b):
-    return (b % 2) * 2 * PIECES + b // 2, 2
+    return (b % 2) * 2 * PIECES + 1 - b // 2, 2
 
 
 def correlate_kernel(skip_hbm, recv_ref, back_ref, skip_ref, sem, stage, blocks, result, partial_rows, out):

time: 49.3 us -> 46.9 us (0.951)
  blocking collectives: 40.8 us -> 38 us
    all_to_all x2, blocking collectives: 40.8 us -> 38 us  [exchange(): lax.all_to_all(blocks, MESH_AXES, 0, 0, axis_index_groups=groups, tiled=T...]
where the time goes in v5:
time: 46.9 us; the launch traced here: 46.3 us
  blocking collectives  38 us (81%)
  Pallas kernels  7.63 us (16%)
  between operations  0.66 us (1%)
    all_to_all x2, blocking collectives, exchange(): lax.all_to_all(blocks, MESH_AXES, 0, 0, axis_index_groups=groups, tiled=T...  38 us
    pallas_call x1, Pallas kernels, shards(): pl.pallas_call(correlate_kernel, out_shape=jax.ShapeDtypeStruct((peers, O...  4.86 us
    pallas_call x1, Pallas kernels, shards(): pl.pallas_call(pack_kernel, out_shape=jax.ShapeDtypeStruct((peers, OWN, 5...  1.96 us

profile of v5, /device:TPU:32, one launch (start us, length us, event | category | flops | bytes accessed | tf_op | source)
XLA Modules:
  0.0 46.3 jit_solution(17028087838918938050)
XLA Ops:
  0.6 2.0 %shard_map.59 = bf16[64,4,640]{2,1,0:T(4,128)(2,1)} custom-call(bf16[256,256]{1,0:T(8,128)(2,1)} %bitcast.5, bf16[256,256]{1,0:T(8,128)(2,1)} %bitcast.6, f32[64,256]{1,0:T(8,128)} %bitcast.7), custom_call_target="tpu_custom_call" | custom-call | tf_op jit(solution)/shard_map/pallas_call | solution.py:211
  2.6 0.0 copy-start
  2.6 22.7 %all_to_all.10.recv_ref = bf16[64,4,640]{2,1,0:T(4,128)(2,1)S(1)} all-to-all(bf16[64,4,640]{2,1,0:T(4,128)(2,1)} %shard_map.59), channel_id=1, replica_groups={{2,0,18,16,34,32,50,48,66,64,82,80,98,96,114,112,130,128,146,144,162,16..., dimensions={0} | all-to-all | bytes 655360 | tf_op jit(solution)/shard_map/all_to_all | solution.py:198
  25.3 0.0 copy-done
  25.3 4.9 %shard_map.60 = bf16[64,4,384]{2,1,0:T(4,128)(2,1)S(1)} custom-call(f32[256]{0:T(256)S(1)} %copy-done, bf16[64,4,640]{2,1,0:T(4,128)(2,1)S(1)} %all_to_all.10.recv_ref), custom_call_target="tpu_custom_call" | custom-call | tf_op jit(solution)/shard_map/pallas_call | solution.py:226
  30.2 15.3 %all_to_all.11.recv_ref = bf16[64,4,384]{2,1,0:T(4,128)(2,1)S(1)} all-to-all(bf16[64,4,384]{2,1,0:T(4,128)(2,1)S(1)} %shard_map.60), channel_id=1, replica_groups={{2,0,18,16,34,32,50,48,66,64,82,80,98,96,114,112,130,128,146,144,162,16..., dimensions={0} | all-to-all | bytes 393216 | tf_op jit(solution)/shard_map/all_to_all | solution.py:198
  45.5 0.8 %shard_map.61 = (bf16[256,256]{1,0:T(8,128)(2,1)}, f32[64,256]{1,0:T(8,128)}) custom-call(bf16[64,4,384]{2,1,0:T(4,128)(2,1)S(1)} %all_to_all.11.recv_ref), custom_call_target="tpu_custom_call" | custom-call | tf_op jit(solution)/shard_map/pallas_call | solution.py:243
Async XLA Ops:
  2.6 22.7 %copy-start = (f32[256]{0:T(256)S(1)}, f32[256]{0:T(256)}, u32[]{:S(2)}) copy-start(f32[256]{0:T(256)} %skip_hbm.1) | copy-start | bytes 3076

commit v6 on v5

--- a/solution.py
+++ b/solution.py
@@ -60,7 +60,7 @@
 
 
 def rows_of(b):
-    return (b % 2) * 2 * PIECES + 1 - b // 2, 2
+    return (1 - b // 2) * 2 * PIECES + (b % 2 + 1 - b // 2) % 2, 2
 
 
 def correlate_kernel(skip_hbm, recv_ref, back_ref, skip_ref, sem, stage, blocks, result, partial_rows, out):

time: 46.9 us -> 46.6 us (level)
  no operation moved by 1% of the time
where the time goes in v6:
time: 46.6 us; the launch traced here: 46.4 us
  blocking collectives  38.1 us (82%)
  Pallas kernels  7.65 us (16%)
  between operations  0.66 us (1%)
    all_to_all x2, blocking collectives, exchange(): lax.all_to_all(blocks, MESH_AXES, 0, 0, axis_index_groups=groups, tiled=T...  38.1 us
    pallas_call x1, Pallas kernels, shards(): pl.pallas_call(correlate_kernel, out_shape=jax.ShapeDtypeStruct((peers, O...  4.88 us
    pallas_call x1, Pallas kernels, shards(): pl.pallas_call(pack_kernel, out_shape=jax.ShapeDtypeStruct((peers, OWN, 5...  1.96 us

profile of v6, /device:TPU:32, one launch (start us, length us, event | category | flops | bytes accessed | tf_op | source)
XLA Modules:
  0.0 46.4 jit_solution(16733593778294409280)
XLA Ops:
  0.6 2.0 %shard_map.59 = bf16[64,4,640]{2,1,0:T(4,128)(2,1)} custom-call(bf16[256,256]{1,0:T(8,128)(2,1)} %bitcast.5, bf16[256,256]{1,0:T(8,128)(2,1)} %bitcast.6, f32[64,256]{1,0:T(8,128)} %bitcast.7), custom_call_target="tpu_custom_call" | custom-call | tf_op jit(solution)/shard_map/pallas_call | solution.py:211
  2.6 0.0 copy-start
  2.6 22.5 %all_to_all.10.recv_ref = bf16[64,4,640]{2,1,0:T(4,128)(2,1)S(1)} all-to-all(bf16[64,4,640]{2,1,0:T(4,128)(2,1)} %shard_map.59), channel_id=1, replica_groups={{2,3,18,19,34,35,50,51,66,67,82,83,98,99,114,115,130,131,146,147,162,16..., dimensions={0} | all-to-all | bytes 655360 | tf_op jit(solution)/shard_map/all_to_all | solution.py:198
  25.1 0.0 copy-done
  25.1 4.9 %shard_map.60 = bf16[64,4,384]{2,1,0:T(4,128)(2,1)S(1)} custom-call(f32[256]{0:T(256)S(1)} %copy-done, bf16[64,4,640]{2,1,0:T(4,128)(2,1)S(1)} %all_to_all.10.recv_ref), custom_call_target="tpu_custom_call" | custom-call | tf_op jit(solution)/shard_map/pallas_call | solution.py:226
  30.0 15.6 %all_to_all.11.recv_ref = bf16[64,4,384]{2,1,0:T(4,128)(2,1)S(1)} all-to-all(bf16[64,4,384]{2,1,0:T(4,128)(2,1)S(1)} %shard_map.60), channel_id=1, replica_groups={{2,3,18,19,34,35,50,51,66,67,82,83,98,99,114,115,130,131,146,147,162,16..., dimensions={0} | all-to-all | bytes 393216 | tf_op jit(solution)/shard_map/all_to_all | solution.py:198
  45.6 0.8 %shard_map.61 = (bf16[256,256]{1,0:T(8,128)(2,1)}, f32[64,256]{1,0:T(8,128)}) custom-call(bf16[64,4,384]{2,1,0:T(4,128)(2,1)S(1)} %all_to_all.11.recv_ref), custom_call_target="tpu_custom_call" | custom-call | tf_op jit(solution)/shard_map/pallas_call | solution.py:243
Async XLA Ops:
  2.6 22.5 %copy-start = (f32[256]{0:T(256)S(1)}, f32[256]{0:T(256)}, u32[]{:S(2)}) copy-start(f32[256]{0:T(256)} %skip_hbm.1) | copy-start | bytes 3076

commit v7 on v6

--- a/solution.py
+++ b/solution.py
@@ -60,7 +60,7 @@
 
 
 def rows_of(b):
-    return (1 - b // 2) * 2 * PIECES + (b % 2 + 1 - b // 2) % 2, 2
+    return (b + 2) % BATCH, BATCH
 
 
 def correlate_kernel(skip_hbm, recv_ref, back_ref, skip_ref, sem, stage, blocks, result, partial_rows, out):

time: 46.6 us -> 46.5 us (level)
  no operation moved by 1% of the time
where the time goes in v7:
time: 46.5 us; the launch traced here: 46.1 us
  blocking collectives  37.8 us (81%)
  Pallas kernels  7.67 us (16%)
  between operations  0.66 us (1%)
    all_to_all x2, blocking collectives, exchange(): lax.all_to_all(blocks, MESH_AXES, 0, 0, axis_index_groups=groups, tiled=T...  37.8 us
    pallas_call x1, Pallas kernels, shards(): pl.pallas_call(correlate_kernel, out_shape=jax.ShapeDtypeStruct((peers, O...  4.9 us
    pallas_call x1, Pallas kernels, shards(): pl.pallas_call(pack_kernel, out_shape=jax.ShapeDtypeStruct((peers, OWN, 5...  1.96 us

profile of v7, /device:TPU:32, one launch (start us, length us, event | category | flops | bytes accessed | tf_op | source)
XLA Modules:
  0.0 46.1 jit_solution(4344300256661791850)
XLA Ops:
  0.6 2.0 %shard_map.59 = bf16[64,4,640]{2,1,0:T(4,128)(2,1)} custom-call(bf16[256,256]{1,0:T(8,128)(2,1)} %bitcast.5, bf16[256,256]{1,0:T(8,128)(2,1)} %bitcast.6, f32[64,256]{1,0:T(8,128)} %bitcast.7), custom_call_target="tpu_custom_call" | custom-call | tf_op jit(solution)/shard_map/pallas_call | solution.py:211
  2.6 0.0 copy-start
  2.6 22.6 %all_to_all.10.recv_ref = bf16[64,4,640]{2,1,0:T(4,128)(2,1)S(1)} all-to-all(bf16[64,4,640]{2,1,0:T(4,128)(2,1)} %shard_map.59), channel_id=1, replica_groups={{2,3,0,1,18,19,16,17,34,35,32,33,50,51,48,49,66,67,64,65,82,83,80,81,98..., dimensions={0} | all-to-all | bytes 655360 | tf_op jit(solution)/shard_map/all_to_all | solution.py:198
  25.2 0.0 copy-done
  25.2 4.9 %shard_map.60 = bf16[64,4,384]{2,1,0:T(4,128)(2,1)S(1)} custom-call(f32[256]{0:T(256)S(1)} %copy-done, bf16[64,4,640]{2,1,0:T(4,128)(2,1)S(1)} %all_to_all.10.recv_ref), custom_call_target="tpu_custom_call" | custom-call | tf_op jit(solution)/shard_map/pallas_call | solution.py:226
  30.1 15.1 %all_to_all.11.recv_ref = bf16[64,4,384]{2,1,0:T(4,128)(2,1)S(1)} all-to-all(bf16[64,4,384]{2,1,0:T(4,128)(2,1)S(1)} %shard_map.60), channel_id=1, replica_groups={{2,3,0,1,18,19,16,17,34,35,32,33,50,51,48,49,66,67,64,65,82,83,80,81,98..., dimensions={0} | all-to-all | bytes 393216 | tf_op jit(solution)/shard_map/all_to_all | solution.py:198
  45.3 0.8 %shard_map.61 = (bf16[256,256]{1,0:T(8,128)(2,1)}, f32[64,256]{1,0:T(8,128)}) custom-call(bf16[64,4,384]{2,1,0:T(4,128)(2,1)S(1)} %all_to_all.11.recv_ref), custom_call_target="tpu_custom_call" | custom-call | tf_op jit(solution)/shard_map/pallas_call | solution.py:243
Async XLA Ops:
  2.6 22.6 %copy-start = (f32[256]{0:T(256)S(1)}, f32[256]{0:T(256)}, u32[]{:S(2)}) copy-start(f32[256]{0:T(256)} %skip_hbm.1) | copy-start | bytes 3076
